TPU v7x, 32 devices: a whole 2x2x4 slice. The times are simulated.
32 devices in a mesh: dp: 4 (over x, core), fsdp: 2 (over y), ctx: 4 (over z).
Axes of the slice: x: 2, y: 2, z: 4, core: 2. Of those that a mesh axis runs over, the one named last changes fastest.
Arguments:
- box_hidden_states: bfloat16 [8, 2048, 8192], P(('dp', 'fsdp'), 'ctx'), may hold values from -60 to 60
- box_token_positions: int32 [8, 2048], P(('dp', 'fsdp')), may hold values from 0 to 8191, as said below
- document_lengths: int32 [8, 3], P(('dp', 'fsdp')), may hold values from 512 to 7168, as said below
- successors: int32 [8, 2048], P(('dp', 'fsdp'), 'ctx'), may hold values from 0 to 2047, as said below
- fixed_key_matrix: bfloat16 [8192, 1024], P('fsdp'), may hold values from -0.0625 to 0.0625
- adapter_down: bfloat16 [8192, 16], replicated, may hold values from -0.0625 to 0.0625
- adapter_up: bfloat16 [16, 1024], replicated, may hold values from -1.5 to 1.5
- pointer_query_map: bfloat16 [1024, 64], replicated, may hold values from -0.1875 to 0.1875
- pointer_key_map: bfloat16 [1024, 64], replicated, may hold values from -0.1875 to 0.1875
Outputs:
- grad_down: float32 [8192, 16], P('fsdp')
- up_gradient: float32 [16, 1024], replicated
- grad_query: float32 [1024, 64], replicated
- grad_key: float32 [1024, 64], replicated
- mean_loss: float32 [], replicated
Inputs may be any that keep to these rules, and one draw needn't show every extreme that they name: `box_token_positions`: each row is increasing; entries k * 512 to (k + 1) * 512 - 1 lie in positions k * 2048 to (k + 1) * 2048 - 1. `document_lengths`: each row holds multiples of 512 that sum to 8192. `successors`: the index of a box token of the same sequence and the same document as the query; the query itself only where it is the document's only box token or so drawn.
All inputs are finite; a program needn't handle non-finite values.
Results may differ from a plain program's by a relative error of at most 0.012.
The roundings to bfloat16 on the way count: a program that leaves them out, or rounds other values in their place, can miss the bound.
Values may be sent and summed in bfloat16 or wider, within the bound.
A program may use at most 128 MiB of HBM per device.

v0:
```python
import math
import jax
import jax.numpy as jnp
from jax import lax
from jax.sharding import PartitionSpec as P

ADAPTER_SCALE = 0.5


def contract_rows(left, right):
    return lax.dot_general(
        left, right, (((0,), (0,)), ((), ())), preferred_element_type=jnp.float32
    )


def contracted_columns(left, right):
    return lax.dot_general(
        left, right, (((1,), (1,)), ((), ())), preferred_element_type=jnp.float32
    )


def precise_rows(left, right):
    return lax.dot_general(
        left.astype(jnp.float32),
        right,
        (((0,), (0,)), ((), ())),
        precision=lax.Precision.HIGHEST,
        preferred_element_type=jnp.float32,
    )


def precise_columns(left, right):
    return lax.dot_general(
        left,
        right.astype(jnp.float32),
        (((1,), (1,)), ((), ())),
        precision=lax.Precision.HIGHEST,
        preferred_element_type=jnp.float32,
    )


def on_device(
    box_hidden_states,
    box_token_positions,
    document_lengths,
    successors,
    fixed_key_matrix,
    adapter_down,
    adapter_up,
    pointer_query_map,
    pointer_key_map,
):
    hidden_states = box_hidden_states[0]
    count = hidden_states.shape[0]
    groups = lax.axis_size("fsdp")
    seqs_all = lax.axis_size("dp") * groups
    ctx_count = lax.axis_size("ctx")
    width = pointer_query_map.shape[1]
    scale = 1.0 / math.sqrt(width)
    pointer_heads = jnp.concatenate([pointer_query_map, pointer_key_map], axis=1)
    adapter_pointer = jnp.dot(adapter_up, pointer_heads, preferred_element_type=jnp.float32).astype(
        jnp.bfloat16
    )
    complete_keys = lax.all_gather(fixed_key_matrix, "fsdp", axis=0, tiled=True)
    pointer_logits = jnp.dot(
        complete_keys, pointer_heads, preferred_element_type=jnp.float32
    ).astype(jnp.bfloat16)
    projected_states = jnp.dot(hidden_states, pointer_logits, preferred_element_type=jnp.float32)
    narrow_rows = jnp.dot(hidden_states, adapter_down, preferred_element_type=jnp.float32).astype(
        jnp.bfloat16
    )
    blended_terms = (
        projected_states
        + ADAPTER_SCALE * jnp.dot(narrow_rows, adapter_pointer, preferred_element_type=jnp.float32)
    ).astype(jnp.bfloat16)
    queries = blended_terms[:, :width]
    keys = blended_terms[:, width:]
    all_keys = lax.all_gather(keys, "ctx", axis=0, tiled=True)
    ends = jnp.cumsum(document_lengths[0])
    segment = jnp.sum(
        (box_token_positions[0][:, None] >= ends[None, :-1]).astype(jnp.int32), axis=1
    )
    own_segment = lax.dynamic_slice_in_dim(segment, lax.axis_index("ctx") * count, count)
    scores = contracted_columns(queries, all_keys) * scale
    same = own_segment[:, None] == segment[None, :]
    masked = jnp.where(same, scores, -jnp.inf)
    top = jnp.max(masked, axis=1, keepdims=True)
    total = jnp.sum(jnp.exp(masked - top), axis=1, keepdims=True)
    lse = top + jnp.log(total)
    column = jnp.arange(scores.shape[1], dtype=jnp.int32)
    hit = column[None, :] == successors[0][:, None]
    picked = jnp.sum(jnp.where(hit, scores, 0.0), axis=1)
    loss_part = jnp.sum(lse[:, 0] - picked)
    prob = jnp.exp(masked - lse)
    weights = ((prob - hit.astype(jnp.float32)) * (scale * (1.0 / seqs_all))).astype(jnp.bfloat16)
    grad_q = jnp.dot(weights, all_keys, preferred_element_type=jnp.float32).astype(jnp.bfloat16)
    grad_k = lax.psum_scatter(
        contract_rows(weights, queries), "ctx", scatter_dimension=0, tiled=True
    ).astype(jnp.bfloat16)
    paired_terms = jnp.concatenate([grad_q, grad_k], axis=1)
    narrow_gradient = (ADAPTER_SCALE * contracted_columns(paired_terms, adapter_pointer)).astype(
        jnp.bfloat16
    )
    projection_gradient = contract_rows(hidden_states, paired_terms)
    narrow_rows_gradient = contract_rows(narrow_rows, paired_terms)
    grad_down = contract_rows(hidden_states, narrow_gradient)
    denominator = seqs_all * count * ctx_count
    rows_each = grad_down.shape[0] // groups
    summed_terms = lax.psum(
        (grad_down, projection_gradient, narrow_rows_gradient, loss_part), ("dp", "fsdp", "ctx")
    )
    head_gradients = precise_rows(complete_keys, summed_terms[1]) + ADAPTER_SCALE * precise_rows(
        adapter_up, summed_terms[2]
    )
    up_gradient = ADAPTER_SCALE * precise_columns(summed_terms[2], pointer_heads)
    down_rows = lax.dynamic_slice_in_dim(
        summed_terms[0], lax.axis_index("fsdp") * rows_each, rows_each, 0
    )
    return (
        down_rows,
        up_gradient,
        head_gradients[:, :width],
        head_gradients[:, width:],
        summed_terms[3] / denominator,
    )


def solution(mesh):
    in_specs = (
        P(("dp", "fsdp"), "ctx", None),
        P(("dp", "fsdp"), None),
        P(("dp", "fsdp"), None),
        P(("dp", "fsdp"), "ctx"),
        P("fsdp", None),
        P(),
        P(),
        P(),
        P(),
    )
    out_specs = (P("fsdp", None), P(), P(), P(), P())
    return jax.shard_map(
        on_device, mesh=mesh, in_specs=in_specs, out_specs=out_specs, check_vma=False
    )
```

profile of v0, /device:TPU:0, one launch (start us, length us, event | category | flops | bytes accessed | tf_op | source)
XLA Modules:
  0.0 445.7 jit_solution(16629726569500244938)
XLA Ops:
  7.2 0.0 all-gather.2.cloned.1.call-start
  7.3 0.7 all-gather.2.cloned.1.call-update
  8.0 0.0 reduce-scatter.2.cloned.1.call-start
  8.0 0.2 reduce-window.4
  8.2 0.1 fusion.24
  8.3 0.1 dynamic_slice.6
  8.4 0.2 convolution_convert_fusion.2
  8.6 5.7 %fusion.15 = bf16[512,16]{0,1:T(8,128)(2,1)S(1)} fusion(bf16[8192,16]{0,1:T(8,128)(2,1)S(1)} %copy-done, bf16[1,512,8192]{2,1,0:T(8,128)(2,1)} %param.9), kind=kOutput, calls=%fused_computation.26 | convolution fusion | flops 134225920 | bytes 8667136 | tf_op jit(solution)/shard_map/dot_general | solution.py:69
  14.3 196.9 %all-gather.2.cloned.1.call-done = bf16[8192,1024]{1,0:T(8,128)(2,1)} async-done(((bf16[4096,1024]{1,0:T(8,128)(2,1)}), bf16[8192,1024]{1,0:T(8,128)(2,1)}) %all-gather.2.cloned.1.call-update) | async-done | bytes 16777232 | tf_op jit(solution)/shard_map/all_gather | solution.py:64
  211.2 13.1 %fusion.10 = f32[512,128]{0,1:T(8,128)S(1)} fusion(bf16[1,512,8192]{2,1,0:T(8,128)(2,1)} %param.9, bf16[1024,128]{0,1:T(8,128)(2,1)S(1)} %constant_dynamic-update-slice_fusion, bf16[8192,1024]{1,0:T(8,128)(2,1)} %all-gather.2.cloned.1.call-done), kind=kOutput, calls=%fused_computation.21 | convolution fusion | flops 3222274048 | bytes 25690112 | tf_op jit(solution)/shard_map/dot_general | solution.py:68
  224.4 0.2 fusion.13
  224.6 13.9 %all_gather.7 = bf16[2048,64]{0,1:T(8,128)(2,1)S(1)} all-gather(bf16[512,64]{0,1:T(8,128)(2,1)S(1)} %slice.22), channel_id=1, replica_groups=mesh['dp'=4,'fsdp'=2,'ctx'=4] {'ctx'}, dimensions={0}, use_global_device_ids=true | all-gather | bytes 327680 | tf_op jit(solution)/shard_map/all_gather | solution.py:78
  238.6 0.9 fusion.6
  239.4 2.1 select_reduce_fusion
  241.5 0.6 subtract_reduce_fusion
  242.1 1.9 multiply_convert_fusion
  244.0 1.3 fusion.19
  245.3 0.0 reduce-scatter.2.cloned.1.call-update
  245.3 0.2 all-reduce.4.cloned.1.call-start
  245.5 0.8 convolution_convert_fusion.1
  246.3 21.2 %reduce-scatter.2.cloned.1.call-done = f32[512,64]{0,1:T(8,128)} async-done(((f32[2048,64]{0,1:T(8,128)}), f32[512,64]{0,1:T(8,128)}) %reduce-scatter.2.cloned.1.call-update) | async-done | bytes 131088 | tf_op jit(solution)/shard_map/reduce_scatter | solution.py:97
  267.5 0.9 convert_element_type.43
  268.4 5.7 %convolution_bitcast_fusion.1 = f32[8192,16]{0,1:T(8,128)} fusion(bf16[1,512,8192]{2,1,0:T(8,128)(2,1)} %param.9, bf16[128,16]{0,1:T(8,128)(2,1)S(1)} %convolution_convert_fusion.2, bf16[512,64]{0,1:T(8,128)(2,1)S(1)} %convert_element_type.43, bf16[512,64]{0,1:T(8,128)(2,1)S(1)} %convolution_convert_fusion.1), kind=kOutput, calls=%fused_computation.2 | convolution fusion | flops 136593408 | bytes 9048064 | tf_op jit(solution)/shard_map/dot_general | solution.py:11
  274.1 6.6 %convolution_bitcast_fusion = f32[8192,128]{0,1:T(8,128)} fusion(bf16[1,512,8192]{2,1,0:T(8,128)(2,1)} %param.9, bf16[512,64]{0,1:T(8,128)(2,1)S(1)} %convert_element_type.43, bf16[512,64]{0,1:T(8,128)(2,1)S(1)} %convolution_convert_fusion.1), kind=kOutput, calls=%fused_computation | convolution fusion | flops 1074003968 | bytes 12713984 | tf_op jit(solution)/shard_map/dot_general | solution.py:11
  280.8 0.1 fusion.23
  280.9 39.2 %all-reduce = (f32[16,128]{1,0:T(8,128)S(1)}, f32[]{:T(128)}) all-reduce(f32[16,128]{1,0:T(8,128)S(1)} %fusion.23, f32[]{:T(128)} %get-tuple-element.11), channel_id=1, replica_groups=mesh['dp'=4,'fsdp'=2,'ctx'=4] {'dp','fsdp','ctx'}, use_global_device_ids=true, to_apply=%region_6.7 | all-reduce | flops 2049 | bytes 16392 | tf_op jit(solution)/shard_map/psum | solution.py:109
  320.7 0.9 convolution_multiply_fusion.3
  321.6 102.4 %all-reduce.4.cloned.1.call-done = (f32[8192,16]{0,1:T(8,128)}, f32[8192,128]{0,1:T(8,128)}) async-done(((f32[8192,16]{0,1:T(8,128)}, f32[8192,128]{0,1:T(8,128)}), (f32[8192,16]{0,1:T(8,128)}, f32[8192,128]{0,1:T(8,128)})) %all-reduce.4.cloned.1.call-update) | async-done | bytes 4718608 | tf_op jit(solution)/shard_map/psum | solution.py:109
  424.0 12.0 %fusion.31 = f32[128,1024]{1,0:T(8,128)S(1)} fusion(f32[8192,128]{0,1:T(8,128)} %get-tuple-element.10, bf16[8192,1024]{1,0:T(8,128)(2,1)} %all-gather.2.cloned.1.call-done), kind=kOutput, calls=%fused_computation.48 | convolution fusion | flops 12884901888 | bytes 21495808 | tf_op jit(solution)/shard_map/dot_general | solution.py:23
  436.1 0.4 fusion.8
  436.5 0.8 fusion.30
  437.3 0.7 constant_dynamic-slice_fusion
  (21 shorter events, 0.1 us)
Async XLA Ops:
  7.2 1.5 copy-start
  7.2 0.8 copy-start.7
  7.2 1.0 copy-start.6
  7.2 1.2 copy-start.3
  7.2 1.2 copy-start.4
  7.2 1.2 copy-start.1
  7.2 204.0 %all-gather.2.cloned.1.call-start = ((), (), s32[]{:S(2)}) async-start(), calls=%async_computation.1 | async-start | bytes 25165824 | tf_op jit(solution)/shard_map/all_gather | solution.py:64
  8.0 259.6 %reduce-scatter.2.cloned.1.call-start = ((), (), s32[]{:S(2)}) async-start(), calls=%async_computation.2 | async-start | bytes 655360 | tf_op jit(solution)/shard_map/reduce_scatter | solution.py:97
  224.4 15.1 %copy-start.5 = (s32[1,512]{1,0:T(1,128)S(1)}, s32[1,512]{1,0:T(1,128)}, u32[]{:S(2)}) copy-start(s32[1,512]{1,0:T(1,128)} %param.12) | copy-start | bytes 6148
  245.3 178.7 %all-reduce.4.cloned.1.call-start = ((), (), s32[]{:S(2)}) async-start(), calls=%async_computation.3 | async-start | bytes 9437184 | tf_op jit(solution)/shard_map/psum | solution.py:109
  424.0 13.3 %copy-start.2 = (f32[8192,16]{0,1:T(8,128)S(1)}, f32[8192,16]{0,1:T(8,128)}, u32[]{:S(2)}) copy-start(f32[8192,16]{0,1:T(8,128)} %get-tuple-element.9) | copy-start | bytes 1572868
Sparse Core Ops, SparseCore 0:
  9.6 201.5 all-gather.1
  245.4 22.0 reduce-scatter.1
  280.9 143.0 all-reduce.3
where the time goes:
time: 446 us
  waiting for transfers between devices  321 us (72%)
  blocking collectives  53.1 us (12%)
  matrix products  47.9 us (11%)
  between operations  15.7 us (4%)
  other arithmetic  5.73 us (1%)
    all_gather x1, waiting for transfers between devices, on_device(): complete_keys = lax.all_gather(fixed_key_matrix, 'fsdp', axis=0, tiled=True)  197 us
    psum x1, waiting for transfers between devices, on_device(): lax.psum((grad_down, projection_gradient, narrow_rows_gradient, loss_part...  102 us
    psum x1, blocking collectives, on_device(): lax.psum((grad_down, projection_gradient, narrow_rows_gradient, loss_part...  39.2 us
    reduce_scatter x1, waiting for transfers between devices, on_device(): lax.psum_scatter(contract_rows(weights, queries), 'ctx', scatter_dimensio...  21.2 us
    all_gather x1, blocking collectives, on_device(): all_keys = lax.all_gather(keys, 'ctx', axis=0, tiled=True)  13.9 us
    dot_general x4, matrix products, contract_rows(): lax.dot_general(left, right, (((0,), (0,)), ((), ())), preferred_element_...  13.7 us
    dot_general x1, matrix products, on_device(): jnp.dot(hidden_states, pointer_logits, preferred_element_type=jnp.float32)  13.1 us
    dot_general x2, matrix products, precise_rows(): lax.dot_general(left.astype(jnp.float32), right, (((0,), (0,)), ((), ()))...  12.5 us
  transfers between devices with their start and end apart: 3, of which 3 were waited for; matrix products, arithmetic and copies ran while one was open for 2% of the time, Pallas kernels for 0%

commit v1 on v0

--- a/solution.py
+++ b/solution.py
@@ -106,9 +106,9 @@
     grad_down = contract_rows(hidden_states, narrow_gradient)
     denominator = seqs_all * count * ctx_count
     rows_each = grad_down.shape[0] // groups
-    summed_terms = lax.psum(
-        (grad_down, projection_gradient, narrow_rows_gradient, loss_part), ("dp", "fsdp", "ctx")
-    )
+    summed_terms = (grad_down, projection_gradient, narrow_rows_gradient, loss_part)
+    for nth in (("fsdp", "ctx"), "dp"):
+        summed_terms = lax.psum(summed_terms, axis_name=nth)
     head_gradients = precise_rows(complete_keys, summed_terms[1]) + ADAPTER_SCALE * precise_rows(
         adapter_up, summed_terms[2]
     )

time: 446 us -> 567 us (1.27)
  waiting for transfers between devices: 321 us -> 453 us
  blocking collectives: 53.1 us -> 42.4 us
    psum x1 -> x2, waiting for transfers between devices: 102 us -> 234 us  [on_device(): summed_terms = lax.psum(summed_terms, axis_name=nth)]
    psum x1 -> x2, blocking collectives: 39.2 us -> 28.5 us  [on_device(): summed_terms = lax.psum(summed_terms, axis_name=nth)]
  transfers between devices with their start and end apart: 3 -> 4, of which waited for: 3 -> 4; matrix products, arithmetic and copies ran while one was open for 2% -> 1% of each run, Pallas kernels for 0% -> 0%
where the time goes in v1:
time: 567 us
  waiting for transfers between devices  453 us (80%)
  matrix products  47.8 us (8%)
  blocking collectives  42.4 us (7%)
  between operations  15.7 us (3%)
  other arithmetic  5.73 us (1%)
    psum x2, waiting for transfers between devices, on_device(): summed_terms = lax.psum(summed_terms, axis_name=nth)  234 us
    all_gather x1, waiting for transfers between devices, on_device(): complete_keys = lax.all_gather(fixed_key_matrix, 'fsdp', axis=0, tiled=True)  197 us
    psum x2, blocking collectives, on_device(): summed_terms = lax.psum(summed_terms, axis_name=nth)  28.5 us
    reduce_scatter x1, waiting for transfers between devices, on_device(): lax.psum_scatter(contract_rows(weights, queries), 'ctx', scatter_dimensio...  21.4 us
    all_gather x1, blocking collectives, on_device(): all_keys = lax.all_gather(keys, 'ctx', axis=0, tiled=True)  13.9 us
    dot_general x4, matrix products, contract_rows(): lax.dot_general(left, right, (((0,), (0,)), ((), ())), preferred_element_...  13.7 us
    dot_general x1, matrix products, on_device(): jnp.dot(hidden_states, pointer_logits, preferred_element_type=jnp.float32)  13.1 us
    dot_general x2, matrix products, precise_rows(): lax.dot_general(left.astype(jnp.float32), right, (((0,), (0,)), ((), ()))...  12.4 us
  transfers between devices with their start and end apart: 4, of which 4 were waited for; matrix products, arithmetic and copies ran while one was open for 1% of the time, Pallas kernels for 0%

profile of v1, /device:TPU:0, one launch (start us, length us, event | category | flops | bytes accessed | tf_op | source)
XLA Modules:
  0.0 566.8 jit_solution(10824941121797738169)
XLA Ops:
  7.3 0.7 all-gather.2.cloned.1.call-update
  8.0 0.2 reduce-window.4
  8.2 0.1 fusion.24
  8.3 0.1 dynamic_slice.6
  8.4 0.2 convolution_convert_fusion.2
  8.6 5.7 fusion.15
  14.3 196.9 %all-gather.2.cloned.1.call-done = bf16[8192,1024]{1,0:T(8,128)(2,1)} async-done(((bf16[4096,1024]{1,0:T(8,128)(2,1)}), bf16[8192,1024]{1,0:T(8,128)(2,1)}) %all-gather.2.cloned.1.call-update) | async-done | bytes 16777232 | tf_op jit(solution)/shard_map/all_gather | solution.py:64
  211.2 13.1 %fusion.10 = f32[512,128]{0,1:T(8,128)S(1)} fusion(bf16[1,512,8192]{2,1,0:T(8,128)(2,1)} %param.9, bf16[1024,128]{0,1:T(8,128)(2,1)S(1)} %constant_dynamic-update-slice_fusion, bf16[8192,1024]{1,0:T(8,128)(2,1)} %all-gather.2.cloned.1.call-done), kind=kOutput, calls=%fused_computation.21 | convolution fusion | flops 3222274048 | bytes 25690112 | tf_op jit(solution)/shard_map/dot_general | solution.py:68
  224.4 0.2 fusion.13
  224.6 13.9 %all_gather.7 = bf16[2048,64]{0,1:T(8,128)(2,1)S(1)} all-gather(bf16[512,64]{0,1:T(8,128)(2,1)S(1)} %slice.22), channel_id=1, replica_groups=mesh['dp'=4,'fsdp'=2,'ctx'=4] {'ctx'}, dimensions={0}, use_global_device_ids=true | all-gather | bytes 327680 | tf_op jit(solution)/shard_map/all_gather | solution.py:78
  238.6 0.9 fusion.6
  239.4 2.1 select_reduce_fusion
  241.5 0.6 subtract_reduce_fusion
  242.1 1.9 multiply_convert_fusion
  244.0 1.3 fusion.19
  245.3 0.0 all-reduce.7.cloned.1.call-start
  245.3 0.8 convolution_convert_fusion.1
  246.1 21.4 %reduce-scatter.2.cloned.1.call-done = f32[512,64]{0,1:T(8,128)} async-done(((f32[2048,64]{0,1:T(8,128)}), f32[512,64]{0,1:T(8,128)}) %reduce-scatter.2.cloned.1.call-update) | async-done | bytes 131088 | tf_op jit(solution)/shard_map/reduce_scatter | solution.py:97
  267.5 0.9 convert_element_type.43
  268.5 5.7 %convolution_bitcast_fusion.1 = f32[8192,16]{0,1:T(8,128)} fusion(bf16[1,512,8192]{2,1,0:T(8,128)(2,1)} %param.9, bf16[128,16]{0,1:T(8,128)(2,1)S(1)} %convolution_convert_fusion.2, bf16[512,64]{0,1:T(8,128)(2,1)S(1)} %convert_element_type.43, bf16[512,64]{0,1:T(8,128)(2,1)S(1)} %convolution_convert_fusion.1), kind=kOutput, calls=%fused_computation.2 | convolution fusion | flops 136593408 | bytes 9048064 | tf_op jit(solution)/shard_map/dot_general | solution.py:11
  274.2 6.6 %convolution_bitcast_fusion = f32[8192,128]{0,1:T(8,128)} fusion(bf16[1,512,8192]{2,1,0:T(8,128)(2,1)} %param.9, bf16[512,64]{0,1:T(8,128)(2,1)S(1)} %convert_element_type.43, bf16[512,64]{0,1:T(8,128)(2,1)S(1)} %convolution_convert_fusion.1), kind=kOutput, calls=%fused_computation | convolution fusion | flops 1074003968 | bytes 12713984 | tf_op jit(solution)/shard_map/dot_general | solution.py:11
  280.8 0.2 all-reduce.9.cloned.1.call-start
  281.0 168.3 %all-reduce.7.cloned.1.call-done = (f32[8192,16]{0,1:T(8,128)}, f32[8192,128]{0,1:T(8,128)}) async-done(((f32[8192,16]{0,1:T(8,128)}, f32[8192,128]{0,1:T(8,128)}), (f32[8192,16]{0,1:T(8,128)}, f32[8192,128]{0,1:T(8,128)})) %all-reduce.7.cloned.1.call-update) | async-done | bytes 4718608 | tf_op jit(solution)/shard_map/psum | solution.py:111
  449.3 0.1 fusion.23
  449.5 20.7 %all-reduce = (f32[16,128]{1,0:T(8,128)S(1)}, f32[]{:T(128)}) all-reduce(f32[16,128]{1,0:T(8,128)S(1)} %fusion.23, f32[]{:T(128)} %get-tuple-element.15), channel_id=1, replica_groups=mesh['dp'=4,'fsdp'=2,'ctx'=4] {'fsdp','ctx'}, use_global_device_ids=true, to_apply=%region_7.8 | all-reduce | flops 2049 | bytes 16392 | tf_op jit(solution)/shard_map/psum | solution.py:111
  470.2 7.8 %all-reduce.2 = (f32[16,128]{1,0:T(8,128)S(1)}, f32[]{:T(128)}) all-reduce(f32[16,128]{1,0:T(8,128)S(1)} %get-tuple-element.7, f32[]{:T(128)} %get-tuple-element.8), channel_id=1, replica_groups=mesh['dp'=4,'fsdp'=2,'ctx'=4] {'dp'}, use_global_device_ids=true, to_apply=%region_8.9 | all-reduce | flops 2049 | bytes 16392 | tf_op jit(solution)/shard_map/psum | solution.py:111
  478.6 0.9 convolution_multiply_fusion.3
  479.5 65.7 %all-reduce.9.cloned.1.call-done = (f32[8192,16]{0,1:T(8,128)}, f32[8192,128]{0,1:T(8,128)}) async-done(((f32[8192,16]{0,1:T(8,128)}, f32[8192,128]{0,1:T(8,128)}), (f32[8192,16]{0,1:T(8,128)}, f32[8192,128]{0,1:T(8,128)})) %all-reduce.9.cloned.1.call-update) | async-done | bytes 4718608 | tf_op jit(solution)/shard_map/psum | solution.py:111
  545.2 12.0 %fusion.31 = f32[128,1024]{1,0:T(8,128)S(1)} fusion(f32[8192,128]{0,1:T(8,128)} %get-tuple-element.14, bf16[8192,1024]{1,0:T(8,128)(2,1)} %all-gather.2.cloned.1.call-done), kind=kOutput, calls=%fused_computation.48 | convolution fusion | flops 12884901888 | bytes 21495808 | tf_op jit(solution)/shard_map/dot_general | solution.py:23
  557.2 0.4 fusion.8
  557.6 0.8 fusion.30
  558.4 0.7 constant_dynamic-slice_fusion
  (25 shorter events, 0.2 us)
Async XLA Ops:
  7.2 1.5 copy-start
  7.2 0.8 copy-start.7
  7.2 1.0 copy-start.6
  7.2 1.2 copy-start.3
  7.2 1.2 copy-start.4
  7.2 1.2 copy-start.1
  7.2 204.0 %all-gather.2.cloned.1.call-start = ((), (), s32[]{:S(2)}) async-start(), calls=%async_computation.1 | async-start | bytes 25165824 | tf_op jit(solution)/shard_map/all_gather | solution.py:64
  8.0 259.6 %reduce-scatter.2.cloned.1.call-start = ((), (), s32[]{:S(2)}) async-start(), calls=%async_computation.2 | async-start | bytes 655360 | tf_op jit(solution)/shard_map/reduce_scatter | solution.py:97
  224.4 15.1 %copy-start.5 = (s32[1,512]{1,0:T(1,128)S(1)}, s32[1,512]{1,0:T(1,128)}, u32[]{:S(2)}) copy-start(s32[1,512]{1,0:T(1,128)} %param.12) | copy-start | bytes 6148
  245.3 204.0 %all-reduce.7.cloned.1.call-start = ((), (), s32[]{:S(2)}) async-start(), calls=%async_computation.3 | async-start | bytes 9437184 | tf_op jit(solution)/shard_map/psum | solution.py:111
  280.8 264.4 %all-reduce.9.cloned.1.call-start = ((), (), s32[]{:S(2)}) async-start(), calls=%async_computation.4 | async-start | bytes 9437184 | tf_op jit(solution)/shard_map/psum | solution.py:111
  545.2 13.3 %copy-start.2 = (f32[8192,16]{0,1:T(8,128)S(1)}, f32[8192,16]{0,1:T(8,128)}, u32[]{:S(2)}) copy-start(f32[8192,16]{0,1:T(8,128)} %get-tuple-element.13) | copy-start | bytes 1572868
Sparse Core Ops, SparseCore 0:
  9.6 201.5 all-gather.1
  245.4 22.0 reduce-scatter.1
  280.9 168.3 all-reduce.6
  451.6 93.5 all-reduce.8
